TPU v7x, 768 devices: a whole 4x8x12 slice. The times are simulated.
768 devices in a mesh: seq: 32 (over y_lo, x, core), tp: 24 (over z, y_hi).
Axes of the slice: x: 4, y: 8 (y_hi: 2, y_lo: 4; y = y_hi * 4 + y_lo), z: 12, core: 2. Of those that a mesh axis runs over, the one named last changes fastest.
Arguments:
- hidden: bfloat16 [4096, 8192], P('seq'), may hold values from -7 to 7
- norm_gain: bfloat16 [8192], replicated, may hold values from 0.099609375 to 1.8984375
- w_query: bfloat16 [8192, 6144], P('seq', 'tp'), may hold values from -1 to 1
- w_key: bfloat16 [8192, 768], P('seq'), may hold values from -64 to 64
- w_value: bfloat16 [8192, 768], P('seq'), may hold values from -0.0625 to 0.0625
- doc_lengths: int32 [8], replicated, may hold values from 1 to 2560, 4096 in all
- critic_up: bfloat16 [8192, 27648], P('seq', 'tp'), may hold values from -0.0625 to 0.0625
- critic_down: bfloat16 [4, 27648, 8192], P(None, 'tp', 'seq'), may hold values from -0.0390625 to 0.0390625
- rule_ids: int32 [8], replicated, may hold values from 0 to 3
Outputs:
- attention: bfloat16 [4096, 6144], P('seq', 'tp')
- critic_values: bfloat16 [8, 8192], P(None, 'seq')
Inputs may be any that keep to these rules, and one draw needn't show every extreme that they name: `doc_lengths`: the 8 lengths sum to 4096; the longest is exactly 2560.
All inputs are finite; a program needn't handle non-finite values.
Results may differ from a plain program's by a relative error of at most 0.03.
The roundings to bfloat16 on the way count: a program that leaves them out, or rounds other values in their place, can miss the bound.
Values may be sent and summed in bfloat16 or wider, within the bound.
A program may use at most 64 MiB of HBM per device.

v0:
```python
import math

import jax
import jax.numpy as jnp
from jax import lax
from jax.sharding import PartitionSpec as P

QH_DEV = 2
GROUP = 8


def rms_norm(values, norm_gain):
    widened = values.astype(jnp.float32)
    mean_square = jnp.mean(widened * widened, axis=-1, keepdims=True)
    return (widened * lax.rsqrt(mean_square + 1e-05) * norm_gain.astype(jnp.float32)).astype(
        jnp.bfloat16
    )


def shards(
    hidden, norm_gain, w_query, w_key, w_value, doc_lengths, critic_up, critic_down, rule_ids
):
    normed = rms_norm(hidden, norm_gain)
    tokens_here = hidden.shape[0]
    head_size = w_query.shape[1] // QH_DEV
    shared_head = lax.axis_index("tp") * QH_DEV // GROUP
    key_columns = lax.dynamic_slice_in_dim(w_key, shared_head * head_size, head_size, 1)
    value_columns = lax.dynamic_slice_in_dim(w_value, shared_head * head_size, head_size, 1)

    def project(weight_rows):
        return jnp.dot(normed, weight_rows, preferred_element_type=jnp.float32)

    query_sum = project(lax.all_gather(w_query, "seq", axis=0, tiled=True))
    key_sum = project(lax.all_gather(key_columns, "seq", axis=0, tiled=True))
    value_sum = project(lax.all_gather(value_columns, "seq", axis=0, tiled=True))
    queries = query_sum.astype(jnp.bfloat16).reshape(tokens_here, QH_DEV, head_size)
    keys = key_sum.astype(jnp.bfloat16)
    values = value_sum.astype(jnp.bfloat16)
    doc_ends = jnp.cumsum(doc_lengths) - 1
    first_row = lax.axis_index("seq") * tokens_here
    query_pos = first_row + jnp.arange(tokens_here, dtype=jnp.int32)

    def segment_of(positions):
        return jnp.sum((positions[:, None] > doc_ends[None, :]).astype(jnp.int32), axis=1)

    query_seg = segment_of(query_pos)
    inverse_root = 1.0 / math.sqrt(head_size)
    maxima = jnp.full((tokens_here, QH_DEV), -1e30, jnp.float32)
    key_block = lax.all_gather(keys, "seq", axis=0, tiled=True)
    value_block = lax.all_gather(values, "seq", axis=0, tiled=True)
    key_pos = jnp.arange(key_block.shape[0], dtype=jnp.int32)
    allowed = (query_seg[:, None] == segment_of(key_pos)[None, :]) & (
        key_pos[None, :] <= query_pos[:, None]
    )
    allowed = allowed[:, None, :]
    scores = (
        jnp.einsum("qhd,kd->qhk", queries, key_block, preferred_element_type=jnp.float32)
        * inverse_root
    )
    scores = jnp.where(allowed, scores, -1e30)
    new_max = jnp.maximum(maxima, jnp.max(scores, axis=2))
    expanded = jnp.where(allowed, jnp.exp(scores - new_max[:, :, None]), 0.0)
    totals = jnp.sum(expanded, axis=2)
    weighted = jnp.einsum(
        "qhk,kd->qhd",
        expanded.astype(jnp.bfloat16),
        value_block,
        preferred_element_type=jnp.float32,
    )
    maxima, totals, weighted = (new_max, totals, weighted)
    attention = (
        (weighted / totals[:, :, None])
        .reshape(tokens_here, QH_DEV * head_size)
        .astype(jnp.bfloat16)
    )
    picker = (doc_ends[:, None] == query_pos[None, :]).astype(jnp.bfloat16)
    end_terms = jnp.dot(picker, normed, preferred_element_type=jnp.float32)
    end_rows = lax.psum_scatter(
        end_terms.astype(jnp.bfloat16), "seq", scatter_dimension=1, tiled=True
    )
    up_terms = jnp.dot(end_rows, critic_up, preferred_element_type=jnp.float32)
    critic_hidden = jax.nn.silu(
        lax.psum(up_terms.astype(jnp.bfloat16), "seq").astype(jnp.float32)
    ).astype(jnp.bfloat16)
    per_rule = jnp.einsum(
        "dc,rce->dre", critic_hidden, critic_down, preferred_element_type=jnp.float32
    )
    rule_pick = (
        rule_ids[:, None] == jnp.arange(critic_down.shape[0], dtype=jnp.int32)[None, :]
    ).astype(jnp.float32)
    chosen = jnp.einsum("dr,dre->de", rule_pick, per_rule)
    critic_values = lax.psum(chosen, "tp").astype(jnp.bfloat16)
    return (attention, critic_values)


def solution(mesh):
    return jax.shard_map(
        shards,
        mesh=mesh,
        in_specs=(
            P("seq", None),
            P(),
            P("seq", "tp"),
            P("seq", None),
            P("seq", None),
            P(),
            P("seq", "tp"),
            P(None, "tp", "seq"),
            P(),
        ),
        out_specs=(P("seq", "tp"), P(None, "seq")),
        check_vma=False,
    )
```

profile of v0, /device:TPU:64, one launch (start us, length us, event | category | flops | bytes accessed | tf_op | source)
XLA Modules:
  0.0 534.5 jit_solution(4791284740765994093)
XLA Ops:
  7.3 1.6 constant_dynamic-slice_fusion.1
  8.9 0.0 all-gather.12.cloned.1.call-start
  9.0 1.5 constant_dynamic-slice_fusion
  10.5 0.0 reduce-scatter.2.cloned.1.call-start
  10.5 0.8 reduce-window.7
  11.3 0.7 convert_element_type.53
  12.1 2.1 fusion.1
  14.2 2.9 convolution_convert_fusion
  17.1 0.0 all-gather.6.cloned.1.call-start
  17.2 0.5 all-gather.6.cloned.1.call-update
  17.7 0.0 all-gather.10.cloned.1.call-start
  17.8 64.8 %all-gather.8.cloned.1.call-done = bf16[8192,128]{1,0:T(8,128)(2,1)} async-done(((bf16[256,128]{1,0:T(8,128)(2,1)}), bf16[8192,128]{1,0:T(8,128)(2,1)}) %all-gather.8.cloned.1.call-update) | async-done | bytes 2097168 | tf_op jit(solution)/shard_map/all_gather | solution.py:34
  82.6 3.6 convolution_convert_fusion.4
  86.2 0.0 all-gather.14.cloned.1.call-start
  86.3 0.1 convert_reduce_fusion.1
  86.4 0.1 convert_reduce_fusion
  86.5 0.1 fusion.34
  86.6 0.5 fusion.10
  87.1 62.6 %all-gather.12.cloned.1.call-done = bf16[8192,128]{1,0:T(8,128)(2,1)} async-done(((bf16[256,128]{1,0:T(8,128)(2,1)}), bf16[8192,128]{1,0:T(8,128)(2,1)}) %all-gather.12.cloned.1.call-update) | async-done | bytes 2097168 | tf_op jit(solution)/shard_map/all_gather | solution.py:35
  149.6 3.9 convolution_convert_fusion.3
  153.6 147.1 %reduce-scatter.2.cloned.1.call-done = bf16[8,256]{1,0:T(8,128)(2,1)} async-done(((bf16[8,8192]{1,0:T(8,128)(2,1)}), bf16[8,256]{1,0:T(8,128)(2,1)}) %reduce-scatter.2.cloned.1.call-update) | async-done | bytes 4112 | tf_op jit(solution)/shard_map/reduce_scatter | solution.py:78
  300.8 0.9 convolution_convert_fusion.1
  301.6 134.3 %psum.14 = bf16[8,1152]{1,0:T(8,128)(2,1)S(1)} all-reduce(bf16[8,1152]{1,0:T(8,128)(2,1)S(1)} %convolution_convert_fusion.1), channel_id=1, replica_groups=mesh['seq'=32,'tp'=24] {'seq'}, use_global_device_ids=true, to_apply=%region_7.8 | all-reduce | flops 9216 | bytes 36864 | tf_op jit(solution)/shard_map/psum | solution.py:83
  435.9 0.4 fusion.30
  436.3 0.1 fusion.27
  436.5 77.9 %psum.15 = bf16[8,256]{1,0:T(8,128)(2,1)} all-reduce(f32[8,256]{1,0:T(8,128)S(1)} %bitcast.34), channel_id=1, replica_groups=mesh['seq'=32,'tp'=24] {'tp'}, use_global_device_ids=true, to_apply=%region_8.9 | all-reduce | flops 2048 | bytes 12288 | tf_op jit(solution)/shard_map/psum | solution.py:92
  514.3 3.6 fusion.12
  518.0 2.3 fusion.44
  520.2 1.9 copy-done.1
  522.2 1.1 fusion.4
  523.3 3.7 fusion.16
  526.9 0.7 copy.14
  (21 shorter events, 0.2 us)
Async XLA Ops:
  7.2 428.8 %copy-start = (bf16[4,1152,256]{2,1,0:T(8,128)(2,1)S(1)}, bf16[4,1152,256]{2,1,0:T(8,128)(2,1)}, u32[]{:S(2)}) copy-start(bf16[4,1152,256]{2,1,0:T(8,128)(2,1)} %param.16) | copy-start | bytes 7077892
  7.2 75.4 %all-gather.8.cloned.1.call-start = ((), (), s32[]{:S(2)}) async-start(), calls=%async_computation.2 | async-start | bytes 2162688 | tf_op jit(solution)/shard_map/all_gather | solution.py:34
  8.9 140.7 %all-gather.12.cloned.1.call-start = ((), (), s32[]{:S(2)}) async-start(), calls=%async_computation.4 | async-start | bytes 2162688 | tf_op jit(solution)/shard_map/all_gather | solution.py:35
  10.5 290.3 %reduce-scatter.2.cloned.1.call-start = ((), (), s32[]{:S(2)}) async-start(), calls=%async_computation.6 | async-start | bytes 135168 | tf_op jit(solution)/shard_map/reduce_scatter | solution.py:78
  14.2 72.3 %copy-start.3 = (s32[8]{0:T(128)S(1)}, s32[8]{0:T(128)}, u32[]{:S(2)}) copy-start(s32[8]{0:T(128)} %param.17) | copy-start | bytes 100
  17.1 497.2 %all-gather.6.cloned.1.call-start = ((), (), s32[]{:S(2)}) async-start(), calls=%async_computation.1 | async-start | bytes 4325376 | tf_op jit(solution)/shard_map/all_gather | solution.py:33
  17.7 283.1 %copy-start.2 = (bf16[256,1152]{1,0:T(8,128)(2,1)S(1)}, bf16[256,1152]{1,0:T(8,128)(2,1)}, u32[]{:S(2)}) copy-start(bf16[256,1152]{1,0:T(8,128)(2,1)} %param.15) | copy-start | bytes 1769476
  17.7 500.2 %all-gather.10.cloned.1.call-start = ((), (), s32[]{:S(2)}) async-start(), calls=%async_computation.3 | async-start | bytes 1081344 | tf_op jit(solution)/shard_map/all_gather | solution.py:49
  86.2 437.0 %all-gather.14.cloned.1.call-start = ((), (), s32[]{:S(2)}) async-start(), calls=%async_computation.5 | async-start | bytes 1081344 | tf_op jit(solution)/shard_map/all_gather | solution.py:50
  520.2 1.9 copy-start.1
Sparse Core Ops, SparseCore 0:
  11.0 71.5 all-gather.7
  85.0 64.5 all-gather.11
  152.7 147.9 reduce-scatter.1
  303.3 64.6 all-gather.5
  371.1 63.2 all-gather.9
  436.9 65.3 all-gather.13
where the time goes:
time: 535 us
  waiting for transfers between devices  275 us (51%)
  blocking collectives  212 us (40%)
  matrix products  21.4 us (4%)
  between operations  14.3 us (3%)
  local copies, waits for them, and re-layouts  5.78 us (1%)
  other arithmetic  5.47 us (1%)
    reduce_scatter x1, waiting for transfers between devices, shards(): lax.psum_scatter(end_terms.astype(jnp.bfloat16), 'seq', scatter_dimension...  147 us
    psum x1, blocking collectives, shards(): lax.psum(up_terms.astype(jnp.bfloat16), 'seq').astype(jnp.float32)  134 us
    psum x1, blocking collectives, shards(): critic_values = lax.psum(chosen, 'tp').astype(jnp.bfloat16)  77.9 us
    all_gather x1, waiting for transfers between devices, shards(): key_sum = project(lax.all_gather(key_columns, 'seq', axis=0, tiled=True))  64.8 us
    all_gather x1, waiting for transfers between devices, shards(): lax.all_gather(value_columns, 'seq', axis=0, tiled=True)  62.6 us
    dot_general x3, matrix products, project(): return jnp.dot(normed, weight_rows, preferred_element_type=jnp.float32)  11.2 us
  transfers between devices with their start and end apart: 6, of which 3 were waited for; matrix products, arithmetic and copies ran while one was open for 5% of the time, Pallas kernels for 0%

commit v1 on v0

v1 whole, which is shorter than its diff:
```python
import math

import jax
import jax.numpy as jnp
from jax import lax
from jax.experimental import pallas as pl
from jax.experimental.pallas import tpu as pltpu
from jax.sharding import PartitionSpec as P

QH_DEV = 2
GROUP = 8
NY, NX, NC = 4, 4, 2
NH = 2
KEY_CHUNK = 4
MESH = pl.DeviceIdType.MESH

EVENTS = (
    (0, 0), (1, 0), (0, -1), (0, 1), (2, 0), (3, 0), (1, -1), (1, 1),
    (2, -1), (2, 1), (3, -1), (3, 1), (0, 2), (1, 2), (2, 2), (3, 2),
)
N_SENDS = 31


def kernel(
    lens, rules, gain, hidden, w_query, w_key, w_value, critic_up, critic_down,
    attention, critic_values,
    hid, nrm, wkv, wq, up, down, kv, acc_kv, acc_q, scores,
    e0, ey, e1, ex, e2, es, u0, uy, u1, ux, u2, us, d0, dh, d1, dz,
    local, wkv_send, wkv_recv, wq_send, wq_recv, kv_send, kv_recv, kvz,
    e_send, e_recv, u_send, u_recv, d_send, d_recv,
):
    n_tp = lax.axis_size("tp")
    n_z = n_tp // NH
    tokens = hid.shape[0]
    docs = lens.shape[0]
    depth = wkv.shape[1]
    n_seq = NY * NX * NC
    s, t = lax.axis_index("seq"), lax.axis_index("tp")
    c, x, y = s % NC, s // NC % NX, s // (NC * NX)
    z, h = t // NH, t % NH

    def row(k):
        return (y // 2 + k // 2) % 2 * 2 + (y + k) % 2

    def slot(ay, ax, ac):
        return (ay * NX + ax) * NC + ac

    def column(dx):
        return (x + dx + NX) % NX

    sib = (slot(y, x, 1 - c), t)
    y_peer = [(slot(row(k), x, c), t) for k in range(NY)]
    x_peer = [(slot(y, column(j), c), t) for j in range(NX)]
    z_mate = (s, (z + 1 - 2 * (z % 2)) * NH + h)
    h_peer = (s, z * NH + 1 - h)
    z_peer = [(s, (z + j) % n_z * NH + h) for j in range(n_z)]

    head = pl.ds(pl.multiple_of((t * QH_DEV // GROUP) * 128, 128), 128)
    key_copy = pltpu.make_async_copy(w_key.at[:, head], wkv.at[s], local.at[0])
    value_copy = pltpu.make_async_copy(w_value.at[:, head], wkv.at[s], local.at[0])

    @pl.when(z % 2 == 0)
    def _():
        key_copy.start()

    @pl.when(z % 2 == 1)
    def _():
        value_copy.start()

    wq_copy = pltpu.make_async_copy(w_query, wq.at[s], local.at[1])
    hid_copy = pltpu.make_async_copy(hidden, hid, local.at[2])
    up_copy = pltpu.make_async_copy(critic_up, up, local.at[3])
    down_copy = pltpu.make_async_copy(critic_down, down, local.at[4])
    for copy in (wq_copy, hid_copy, up_copy, down_copy):
        copy.start()

    barrier = pltpu.get_barrier_semaphore()
    partners = [sib, *y_peer[1:], *x_peer[1:], h_peer, *z_peer[1:]]
    for partner in partners:
        pl.semaphore_signal(barrier, inc=1, device_id=partner, device_id_type=MESH)
    pl.semaphore_wait(barrier, len(partners))

    sends = []

    def remote(src, dst, send_sem, recv_sem, device):
        return pltpu.make_async_remote_copy(
            src_ref=src, dst_ref=dst, send_sem=send_sem, recv_sem=recv_sem,
            device_id=device, device_id_type=MESH,
        )

    def send(*args):
        copy = remote(*args)
        copy.start()
        sends.append(copy)

    def gather(buf, send_sems, recv_sems):
        def go(a, device, i):
            send(buf.at[a], buf.at[a], send_sems.at[i], recv_sems.at[a], device)

        def got(a):
            remote(buf.at[a], buf.at[a], send_sems.at[0], recv_sems.at[a], sib).wait_recv()

        def own(i):
            k, dx = EVENTS[i]
            a = slot(row(k), column(dx), c)
            if i > 0:
                got(a)
            else:
                for j in range(1, NY):
                    go(a, y_peer[j], j - 1)
            if dx == 0:
                go(a, x_peer[1], 3 + k)
                go(a, x_peer[3], 7 + k)
            if dx == -1 and k % 2 == 0:
                go(a, x_peer[1], 11 + k // 2)
            if dx == 1 and k % 2 == 1:
                go(a, x_peer[3], 13 + k // 2)
            go(a, sib, 15 + i)
            return a

        def other(i):
            k, dx = EVENTS[i]
            a = slot(row(k), column(dx), 1 - c)
            got(a)
            return a

        return own, other

    kvw_own, kvw_other = gather(wkv, wkv_send, wkv_recv)
    q_own, q_other = gather(wq, wq_send, wq_recv)
    value_copy.wait()
    kvw_own(0)
    wq_copy.wait()
    q_own(0)

    hid_copy.wait()
    wide_gain = gain[...].astype(jnp.float32)

    def norm_rows(i, carry):
        rows = pl.ds(pl.multiple_of(i * 16, 16), 16)
        wide = hid[rows, :].astype(jnp.float32)
        mean_square = jnp.mean(wide * wide, axis=-1, keepdims=True)
        normed = (wide * lax.rsqrt(mean_square + 1e-05) * wide_gain).astype(jnp.bfloat16)
        for a in range(n_seq):
            nrm[a, rows, :] = normed[:, a * depth : (a + 1) * depth]
        return carry

    lax.fori_loop(0, tokens // 16, norm_rows, 0)

    ends, run = [], 0
    for d in range(docs):
        run = run + lens[d]
        ends.append(run - 1)
    first = s * tokens
    doc_of = lax.broadcasted_iota(jnp.int32, (docs, tokens), 0)
    ends_vec = jnp.zeros((docs, tokens), jnp.int32)
    for d in range(docs):
        ends_vec = jnp.where(doc_of == d, ends[d], ends_vec)
    here = lax.broadcasted_iota(jnp.int32, (docs, tokens), 1) + first
    picker = (ends_vec == here).astype(jnp.float32).astype(jnp.bfloat16)

    def pick(a, carry):
        e0[a] = jnp.dot(picker, nrm[a], preferred_element_type=jnp.float32)
        return carry

    lax.fori_loop(0, n_seq, pick, 0)
    per_y = NX * NC
    for k in range(1, NY):
        send(
            e0.at[pl.ds(row(k) * per_y, per_y)], ey.at[k - 1], e_send.at[k - 1], e_recv.at[k - 1],
            y_peer[k],
        )

    def wait_for(ref, recv_sem, send_sem):
        remote(ref, ref, send_sem, recv_sem, sib).wait_recv()

    def end_rows_y():
        for k in range(NY - 1):
            wait_for(ey.at[k], e_recv.at[k], e_send.at[0])
        e1[...] = e0[pl.ds(y * per_y, per_y)] + ey[0] + ey[1] + ey[2]
        for j in range(1, NX):
            send(
                e1.at[pl.ds(column(j) * NC, NC)], ex.at[j - 1], e_send.at[2 + j], e_recv.at[2 + j],
                x_peer[j],
            )

    def end_rows_x():
        for j in range(NX - 1):
            wait_for(ex.at[j], e_recv.at[3 + j], e_send.at[0])
        e2[...] = e1[pl.ds(x * NC, NC)] + ex[0] + ex[1] + ex[2]
        send(e2.at[1 - c], es, e_send.at[6], e_recv.at[6], sib)

    def up_terms():
        wait_for(es, e_recv.at[6], e_send.at[0])
        end_rows = (e2[c] + es[...]).astype(jnp.bfloat16)
        up_copy.wait()
        u0[...] = jnp.dot(end_rows, up[...], preferred_element_type=jnp.float32)
        for k in range(1, NY):
            send(u0, uy.at[k - 1], u_send.at[k - 1], u_recv.at[k - 1], y_peer[k])

    def up_y():
        for k in range(NY - 1):
            wait_for(uy.at[k], u_recv.at[k], u_send.at[0])
        u1[...] = u0[...] + uy[0] + uy[1] + uy[2]
        for j in range(1, NX):
            send(u1, ux.at[j - 1], u_send.at[2 + j], u_recv.at[2 + j], x_peer[j])

    def up_x():
        for j in range(NX - 1):
            wait_for(ux.at[j], u_recv.at[3 + j], u_send.at[0])
        u2[...] = u1[...] + ux[0] + ux[1] + ux[2]
        send(u2, us, u_send.at[6], u_recv.at[6], sib)

    def down_terms():
        wait_for(us, u_recv.at[6], u_send.at[0])
        v = u2[...] + us[...]
        critic_hidden = v / (1.0 + jnp.exp(-v))
        doc = lax.broadcasted_iota(jnp.int32, critic_hidden.shape, 0)
        rule = jnp.zeros(critic_hidden.shape, jnp.int32)
        for d in range(docs):
            rule = jnp.where(doc == d, rules[d], rule)
        down_copy.wait()
        total = None
        for r in range(down.shape[0]):
            mine = jnp.where(rule == r, critic_hidden, 0.0).astype(jnp.bfloat16)
            term = jnp.dot(mine, down[r], preferred_element_type=jnp.float32)
            total = term if total is None else total + term
        d0[...] = total
        send(d0, dh, d_send.at[0], d_recv.at[n_z], h_peer)

    def down_h():
        wait_for(dh, d_recv.at[n_z], d_send.at[0])
        both = d0[...] + dh[...]
        d1[...] = both
        dz[z] = both
        for j in range(1, n_z):
            send(d1, dz.at[z], d_send.at[j], d_recv.at[z], z_peer[j])

    def down_z():
        for j in range(1, n_z):
            there = (z + j) % n_z
            wait_for(dz.at[there], d_recv.at[there], d_send.at[0])
        total = dz[0]
        for a in range(1, n_z):
            total = total + dz[a]
        critic_values[...] = total.astype(jnp.bfloat16)

    acc_kv[...] = jnp.zeros_like(acc_kv)
    acc_q[...] = jnp.zeros_like(acc_q)

    def use_kv(a):
        acc_kv[...] += jnp.dot(nrm[a], wkv[a], preferred_element_type=jnp.float32)

    def use_q(a):
        acc_q[...] += jnp.dot(nrm[a], wq[a], preferred_element_type=jnp.float32)

    n_events = len(EVENTS)
    use_kv(s)
    stages = {5: end_rows_y, 9: end_rows_x, 13: up_terms}
    for i in range(1, n_events):
        use_kv(kvw_own(i))
        if i >= 2:
            use_kv(kvw_other(i - 2))
        if i in stages:
            stages[i]()
    use_kv(kvw_other(n_events - 2))
    use_kv(kvw_other(n_events - 1))
    kind = z % 2
    kv[s, kind] = acc_kv[...].astype(jnp.bfloat16)
    send(kv.at[s, kind], kv.at[s, kind], kvz.at[0], kvz.at[1], z_mate)

    kv_own, kv_other = gather(kv, kv_send, kv_recv)
    use_q(s)
    stages = {3: up_y, 6: up_x, 9: down_terms, 12: down_h}
    lead = 4
    for i in range(1, n_events + lead):
        if i < n_events:
            use_q(q_own(i))
            if i >= 2:
                use_q(q_other(i - 2))
        if i == lead:
            wait_for(kv.at[s, 1 - kind], kvz.at[1], kvz.at[0])
        if i >= lead:
            kv_own(i - lead)
        if i in stages:
            stages[i]()
    use_q(q_other(n_events - 2))
    use_q(q_other(n_events - 1))
    for i in range(n_events):
        kv_other(i)

    queries = acc_q[...].astype(jnp.bfloat16)
    stacked = jnp.concatenate([queries[:, :128], queries[:, 128:]], axis=0)
    rows = QH_DEV * tokens
    position = lax.broadcasted_iota(jnp.int32, (rows, 1), 0) % tokens + first
    start = jnp.zeros((rows, 1), jnp.int32)
    for d in range(docs):
        start = jnp.maximum(start, jnp.where(ends[d] < position, ends[d] + 1, 0))
    chunk = KEY_CHUNK * tokens
    chunks = s // KEY_CHUNK + 1
    inverse_root = 1.0 / math.sqrt(128)

    def score(i, maxima):
        keys = kv[pl.ds(i * KEY_CHUNK, KEY_CHUNK), 0].reshape(chunk, 128)
        found = lax.dot_general(
            stacked, keys, (((1,), (1,)), ((), ())), preferred_element_type=jnp.float32
        )
        there = lax.broadcasted_iota(jnp.int32, (rows, chunk), 1) + i * chunk
        allowed = (there >= start) & (there <= position)
        found = jnp.where(allowed, found * inverse_root, -1e30)
        scores[i] = found
        return jnp.maximum(maxima, jnp.max(found, axis=1, keepdims=True))

    maxima = lax.fori_loop(0, chunks, score, jnp.full((rows, 1), -1e30, jnp.float32))

    def mix(i, carry):
        totals, mixed = carry
        values = kv[pl.ds(i * KEY_CHUNK, KEY_CHUNK), 1].reshape(chunk, 128)
        weights = jnp.exp(scores[i] - maxima)
        totals = totals + jnp.sum(weights, axis=1, keepdims=True)
        mixed = mixed + jnp.dot(
            weights.astype(jnp.bfloat16), values, preferred_element_type=jnp.float32
        )
        return totals, mixed

    totals, mixed = lax.fori_loop(
        0, chunks, mix, (jnp.zeros((rows, 1), jnp.float32), jnp.zeros((rows, 128), jnp.float32))
    )
    out = (mixed / totals).astype(jnp.bfloat16)
    attention[:, :128] = out[:tokens]
    attention[:, 128:] = out[tokens:]
    down_z()
    for copy in sends:
        copy.wait_send()


def shards(
    hidden, norm_gain, w_query, w_key, w_value, doc_lengths, critic_up, critic_down, rule_ids
):
    tokens, width = hidden.shape
    depth, q_columns = w_query.shape
    rules, hidden_units, out_columns = critic_down.shape
    docs = doc_lengths.shape[0]
    n_seq = NY * NX * NC
    n_z = lax.axis_size("tp") // NH
    bf16, f32 = jnp.bfloat16, jnp.float32
    vmem, dma = pltpu.VMEM, pltpu.SemaphoreType.DMA
    anywhere = pl.BlockSpec(memory_space=pl.ANY)
    return pl.pallas_call(
        kernel,
        out_shape=(
            jax.ShapeDtypeStruct((tokens, q_columns), bf16),
            jax.ShapeDtypeStruct((docs, out_columns), bf16),
        ),
        in_specs=[
            pl.BlockSpec(memory_space=pltpu.SMEM),
            pl.BlockSpec(memory_space=pltpu.SMEM),
            pl.BlockSpec(memory_space=pltpu.VMEM),
            *[anywhere] * 6,
        ],
        out_specs=(pl.BlockSpec(memory_space=pltpu.VMEM), pl.BlockSpec(memory_space=pltpu.VMEM)),
        scratch_shapes=[
            vmem((tokens, width), bf16),
            vmem((n_seq, tokens, depth), bf16),
            vmem((n_seq, depth, 128), bf16),
            vmem((n_seq, depth, q_columns), bf16),
            vmem(critic_up.shape, bf16),
            vmem(critic_down.shape, bf16),
            vmem((n_seq, 2, tokens, 128), bf16),
            vmem((tokens, 128), f32),
            vmem((tokens, q_columns), f32),
            vmem((n_seq // KEY_CHUNK, QH_DEV * tokens, KEY_CHUNK * tokens), f32),
            vmem((n_seq, docs, depth), f32),
            vmem((NY - 1, NX * NC, docs, depth), f32),
            vmem((NX * NC, docs, depth), f32),
            vmem((NX - 1, NC, docs, depth), f32),
            vmem((NC, docs, depth), f32),
            vmem((docs, depth), f32),
            vmem((docs, hidden_units), f32),
            vmem((NY - 1, docs, hidden_units), f32),
            vmem((docs, hidden_units), f32),
            vmem((NX - 1, docs, hidden_units), f32),
            vmem((docs, hidden_units), f32),
            vmem((docs, hidden_units), f32),
            vmem((docs, out_columns), f32),
            vmem((docs, out_columns), f32),
            vmem((docs, out_columns), f32),
            vmem((n_z, docs, out_columns), f32),
            dma((5,)),
            dma((N_SENDS,)),
            dma((n_seq,)),
            dma((N_SENDS,)),
            dma((n_seq,)),
            dma((N_SENDS,)),
            dma((n_seq,)),
            dma((2,)),
            dma((7,)),
            dma((7,)),
            dma((7,)),
            dma((7,)),
            dma((n_z,)),
            dma((n_z + 1,)),
        ],
        compiler_params=pltpu.CompilerParams(
            collective_id=0, has_side_effects=True, vmem_limit_bytes=60 * 1024 * 1024
        ),
        cost_estimate=pl.CostEstimate(
            flops=2 * 10**9, bytes_accessed=8 * 2**20, transcendentals=2**20
        ),
    )(
        doc_lengths, rule_ids, norm_gain.reshape(1, width), hidden, w_query, w_key, w_value,
        critic_up, critic_down,
    )


def solution(mesh):
    return jax.shard_map(
        shards,
        mesh=mesh,
        in_specs=(
            P("seq", None),
            P(),
            P("seq", "tp"),
            P("seq", None),
            P("seq", None),
            P(),
            P("seq", "tp"),
            P(None, "tp", "seq"),
            P(),
        ),
        out_specs=(P("seq", "tp"), P(None, "seq")),
        check_vma=False,
    )
```

time: 535 us -> 93 us (0.17)
  the two profiles are of different devices: /device:TPU:64 before, /device:TPU:63 now
where the time goes in v1:
time: 93 us; the launch traced here: 92.7 us
  Pallas kernels  88 us (95%)
  local copies, waits for them, and re-layouts  4.1 us (4%)
    pallas_call x1, Pallas kernels, shards(): pl.pallas_call(kernel, out_shape=(jax.ShapeDtypeStruct((tokens, q_columns...  88 us
    unnamed x2, local copies, waits for them, and re-layouts  2.74 us

profile of v1, /device:TPU:63, one launch (start us, length us, event | category | flops | bytes accessed | tf_op | source)
XLA Modules:
  0.0 92.7 jit_solution(12050940041134509828)
XLA Ops:
  0.6 1.4 %reshape.7.gain = bf16[1,8192]{1,0:T(2,128)(2,1)} reshape(bf16[8192]{0:T(1024)(128)(2,1)} %param.10) | data formatting | bytes 32768 | tf_op jit(solution)/shard_map/reshape | solution.py:411
  2.0 88.0 %shard_map.104 = (bf16[128,256]{1,0:T(8,128)(2,1)}, bf16[8,256]{1,0:T(8,128)(2,1)}) custom-call(s32[8]{0:T(128)} %lens.1, s32[8]{0:T(128)} %rules.1, bf16[1,8192]{1,0:T(2,128)(2,1)} %reshape.7.gain, bf16[128,8192]{1,0:T(8,128)(2,1)} %hidden.1, bf16[256,256]{1,0:T(8,128)(2,1)} %w_query.1, bf16[256,768]{1,0:T(8,128)(2,1)} %w_key.1, bf16[256,768]{1,0:T(8,128)(2,1)} %w_value.1, ...), custom_call_target="tpu_custom_call" | custom-call | flops 2000000000 | bytes 8388608 | tf_op jit(solution)/shard_map/pallas_call | solution.py:349
  90.0 1.5 %copy.13 = bf16[128,256]{1,0:T(8,128)(2,1)} copy(bf16[128,256]{1,0:T(8,128)(2,1)} %get-tuple-element.4) | data formatting | bytes 131072
  91.4 1.3 %copy.14 = bf16[8,256]{1,0:T(8,128)(2,1)} copy(bf16[8,256]{1,0:T(8,128)(2,1)} %get-tuple-element.5) | data formatting | bytes 8192

commit v2 on v1

v2 whole, which is shorter than its diff:
```python
import functools
import math

import jax
import jax.numpy as jnp
from jax import lax
from jax.experimental import pallas as pl
from jax.experimental.pallas import tpu as pltpu
from jax.sharding import PartitionSpec as P

QH_DEV = 2
GROUP = 8
NY, NX, NC = 4, 4, 2
NH = 2
KEY_CHUNK = 4
MESH = pl.DeviceIdType.MESH

LINE_EVENTS = (
    (0, 0), (1, 0), (0, -1), (0, 1), (2, 0), (3, 0), (1, -1), (1, 1),
    (2, -1), (2, 1), (3, -1), (3, 1), (0, 2), (1, 2), (2, 2), (3, 2),
)
RING_EVENTS = (
    (0, 0), (-1, 0), (1, 0), (0, -1), (0, 1), (2, 0), (-1, -1), (-1, 1),
    (1, -1), (1, 1), (2, -1), (2, 1), (0, 2), (1, 2), (-1, 2), (2, 2),
)
N_SENDS = 32
SCHEDULE = (
    "w0", "q0", "ends", "w1", "w2", "w3", "late", "norm", "ey", "w4", "w5", "q1", "w6", "q2", "w7", "w8", "q3", "w9",
    "q4", "ex", "up", "w10", "w11", "q5", "w12", "both", "w13", "w14", "w15", "kpart", "uy", "q6", "q7", "kown", "ux",
    "z", "k0", "v0", "q8", "q9", "down", "k1", "k2", "q10", "v1", "v2", "q11", "v3", "q12", "q13", "k3", "k4", "k5",
    "v4", "k6", "q14", "v5", "k7", "v6", "dh", "q15", "qpart", "k8", "v7", "k9", "v8", "k10", "k11", "v9", "k12",
    "v10", "v11", "v12", "qown", "a0", "k13", "v13", "v14", "k14", "a1", "k15", "v15", "a2", "a3", "dz",
)


def kernel(
    lens, rules, gain, hidden, w_query, w_key, w_value, critic_up, critic_down,
    attention, critic_values,
    hid, both, outbox, wkv, wq, up, down, kv, acc_kv, part_kv, acc_q, part_q, stacked, maxima, totals, mixed,
    e0, ey, e1, ex, e2, es, picked, u0, uy, u1, ux, u2, us, d0, dh, d1, dz,
    local, w_send, w_recv, q_send, q_recv, k_send, k_recv, v_send, v_recv, kvz, swap,
    e_send, e_recv, u_send, u_recv, d_send, d_recv,
):
    f32, bf16 = jnp.float32, jnp.bfloat16
    n_z = lax.axis_size("tp") // NH
    tokens, width = hid.shape
    docs = lens.shape[0]
    depth = wkv.shape[1]
    n_seq = NY * NX * NC
    s, t = lax.axis_index("seq"), lax.axis_index("tp")
    c, x, y = s % NC, s // NC % NX, s // (NC * NX)
    z, h = t // NH, t % NH
    tall = h * NY + y
    here = y * NX + x

    def row(k):
        return (y // 2 + k // 2) % 2 * 2 + (y + k) % 2

    def slot(ay, ax, ac):
        return (ay * NX + ax) * NC + ac

    def column(dx):
        return (x + dx + NX) % NX

    def up_by(dy):
        there = (tall + dy + NH * NY) % (NH * NY)
        return (slot(there % NY, x, c), z * NH + there // NY)

    sib = (slot(y, x, 1 - c), t)
    y_peer = [(slot(row(k), x, c), t) for k in range(NY)]
    x_peer = [(slot(y, column(j), c), t) for j in range(NX)]
    x_next, x_back, y_next, y_back = x_peer[1], x_peer[3], up_by(1), up_by(-1)
    z_mate = (s, (z + 1 - 2 * (z % 2)) * NH + h)
    h_peer = up_by(NY)
    z_peer = [(s, (z + j) % n_z * NH + h) for j in range(n_z)]

    head = pl.ds(pl.multiple_of((t * QH_DEV // GROUP) * 128, 128), 128)
    key_copy = pltpu.make_async_copy(w_key.at[:, head], wkv.at[here], local.at[0])
    value_copy = pltpu.make_async_copy(w_value.at[:, head], wkv.at[here], local.at[0])

    @pl.when(z % 2 == 0)
    def _():
        key_copy.start()

    @pl.when(z % 2 == 1)
    def _():
        value_copy.start()

    wq_copy = pltpu.make_async_copy(w_query, wq.at[here], local.at[1])
    hid_copy = pltpu.make_async_copy(hidden, hid, local.at[2])
    up_copy = pltpu.make_async_copy(critic_up, up, local.at[3])
    down_copy = pltpu.make_async_copy(critic_down, down, local.at[4])
    for copy in (wq_copy, hid_copy):
        copy.start()

    barrier = pltpu.get_barrier_semaphore()
    partners = [
        sib, *y_peer[1:], *x_peer[1:], y_next, y_back, up_by(2), up_by(-2), h_peer, *z_peer[1:],
    ]
    for partner in partners:
        pl.semaphore_signal(barrier, inc=1, device_id=partner, device_id_type=MESH)
    pl.semaphore_wait(barrier, len(partners))

    sends = []

    def remote(src, dst, send_sem, recv_sem, device):
        return pltpu.make_async_remote_copy(
            src_ref=src, dst_ref=dst, send_sem=send_sem, recv_sem=recv_sem,
            device_id=device, device_id_type=MESH,
        )

    def send(*args, when=None):
        copy = remote(*args)
        sends.append((copy, when))
        if when is None:
            copy.start()
        else:
            pl.when(when)(copy.start)

    def wait_for(ref, recv_sem, send_sem):
        remote(ref, ref, send_sem, recv_sem, sib).wait_recv()

    def mover(buf, send_sems, recv_sems):
        used = []

        def go(a, device, part=None, when=None):
            ref = buf.at[a] if part is None else buf.at[a, part]
            send(ref, ref, send_sems.at[len(used)], recv_sems.at[a], device, when=when)
            used.append(a)

        def got(a):
            wait_for(buf.at[a], recv_sems.at[a], send_sems.at[0])

        return go, got

    upper = y // 2
    inner_row = y + upper * (3 - 2 * y)
    inside = inner_row == 1
    inward = (slot(y + 1 - 2 * upper, x, c), t)
    outward = (slot((y - 1 + 2 * upper + NY) % NY, x, c), t)

    def line_gather(buf, send_sems, recv_sems):
        go, got = mover(buf, send_sems, recv_sems)

        def line_row(e):
            there = (inner_row, 1 - inner_row, 2, 3)[e]
            return there + upper * (3 - 2 * there)

        def own(i):
            e, dx = LINE_EVENTS[i]
            a = line_row(e) * NX + column(dx)
            if i > 0:
                got(a)
            if dx == 0:
                if e == 0:
                    go(a, inward)
                if e == 1:
                    go(a, inward, when=inside)
                else:
                    go(a, outward, when=inside)
            if dx == 0 or (dx == -1 and e % 2 == 0):
                go(a, x_next)
            if dx == 0 or (dx == 1 and e % 2 == 1):
                go(a, x_back)
            return a

        return own

    def ring_gather(buf, send_sems, recv_sems, x_first, cores):
        go, got = mover(buf, send_sems, recv_sems)
        near, far = ((x_next, x_back), (y_next, y_back)) if x_first else ((y_next, y_back), (x_next, x_back))
        half = buf.shape[1] // 2

        def place(a, b, core):
            dx, dy = (a, b) if x_first else (b, a)
            at = (y + dy + NY) % NY * NX + column(dx)
            return at * NC + core if cores else at

        def own(i):
            a, b = RING_EVENTS[i]
            shard = place(a, b, c)
            if i > 0:
                got(shard)
            if b == 0:
                if a == 0:
                    go(shard, near[0])
                    go(shard, near[1])
                if a == -1:
                    go(shard, near[0], pl.ds(0, half))
                if a == 1:
                    go(shard, near[1], pl.ds(half, half))
            if b == 0 or (b == -1 and a in (0, 1)):
                go(shard, far[0])
            if b == 0 or (b == 1 and a in (-1, 2)):
                go(shard, far[1])
            if cores:
                go(shard, sib)
            return shard

        def other(i):
            shard = place(*RING_EVENTS[i], 1 - c)
            got(shard)
            return shard

        return own, other

    w_own, _ = ring_gather(wkv, w_send, w_recv, False, False)
    q_own = line_gather(wq, q_send, q_recv)
    k_own, k_other = ring_gather(kv.at[0], k_send, k_recv, True, True)
    v_own, v_other = ring_gather(kv.at[1], v_send, v_recv, True, True)
    n_events = len(RING_EVENTS)

    acc_kv[...] = jnp.zeros_like(acc_kv)
    acc_q[...] = jnp.zeros_like(acc_q)

    ends, run = [], 0
    for d in range(docs):
        run = run + lens[d]
        ends.append(run - 1)
    first = s * tokens
    wide_gain = gain[...].reshape(1, width).astype(f32)

    def rms(wide, gains):
        mean_square = jnp.mean(wide * wide, axis=-1, keepdims=True)
        return (wide * lax.rsqrt(mean_square + 1e-05) * gains).astype(bf16)

    def norm():
        def norm_rows(i, carry):
            rows = pl.ds(pl.multiple_of(i * 16, 16), 16)
            normed = rms(hid[rows, :].astype(f32), wide_gain)
            for a in range(n_seq // NC):
                pair = [normed[:, (a * NC + core) * depth : (a * NC + core + 1) * depth] for core in range(NC)]
                both[a, c, rows, :] = jnp.where(c == 0, pair[0], pair[1])
                outbox[a, rows, :] = jnp.where(c == 0, pair[1], pair[0])
            return carry

        lax.fori_loop(0, tokens // 16, norm_rows, 0)
        send(outbox, both.at[:, c], swap.at[0], swap.at[1], sib)

    def other_rows():
        wait_for(outbox, swap.at[1], swap.at[0])

    def late():
        up_copy.start()
        down_copy.start()

    def end_rows():
        hid_copy.wait()
        doc = lax.broadcasted_iota(jnp.int32, (docs, tokens), 0)
        doc_end = jnp.zeros((docs, tokens), jnp.int32)
        for d in range(docs):
            doc_end = jnp.where(doc == d, ends[d], doc_end)
        place_here = lax.broadcasted_iota(jnp.int32, (docs, tokens), 1) + first
        picker = (doc_end == place_here).astype(f32).astype(bf16)
        step = 1024

        def columns(i, carry):
            part = pl.ds(pl.multiple_of(i * step, step), step)
            picked[:, part] = jnp.dot(picker, hid[:, part], preferred_element_type=f32)
            return carry

        lax.fori_loop(0, width // step, columns, 0)
        normed = rms(picked[...], wide_gain).astype(f32)
        for ay in range(NY):
            for ax in range(NX):
                at = slot(ay, ax, 0) * depth
                pair = [normed[:, at + core * depth : at + (core + 1) * depth] for core in range(NC)]
                e0[ay, ax] = jnp.concatenate(pair, axis=0).astype(bf16)
        for j, device in enumerate((y_next, up_by(2), y_back)):
            send(e0.at[(y + j + 1) % NY], ey.at[j], e_send.at[j], e_recv.at[j], device)

    def add(parts):
        total = parts[0].astype(f32)
        for part in parts[1:]:
            total = total + part.astype(f32)
        return total

    def end_rows_y():
        for k in range(NY - 1):
            wait_for(ey.at[k], e_recv.at[k], e_send.at[0])
        e1[...] = add([e0[y], *(ey[k] for k in range(NY - 1))]).astype(bf16)
        for j in range(1, NX):
            send(e1.at[column(j)], ex.at[j - 1], e_send.at[2 + j], e_recv.at[2 + j], x_peer[j])

    def end_rows_x():
        for j in range(NX - 1):
            wait_for(ex.at[j], e_recv.at[3 + j], e_send.at[0])
        e2[...] = add([e1[x], *(ex[j] for j in range(NX - 1))]).astype(bf16)
        send(e2, es, e_send.at[6], e_recv.at[6], sib)

    units = up.shape[1]
    wide_half = u0.shape[1]

    def up_terms():
        wait_for(es, e_recv.at[6], e_send.at[0])
        pair = add([e2[...], es[...]])
        end_row = jnp.where(c == 0, pair[:docs], pair[docs:]).astype(bf16)
        up_copy.wait()
        terms = jnp.dot(end_row, up[...], preferred_element_type=f32)
        pad = jnp.zeros((docs, 2 * wide_half - units), f32)
        lower = jnp.concatenate([terms[:, wide_half:], pad], axis=1)
        u0[...] = jnp.concatenate([terms[:, :wide_half], lower], axis=0).astype(bf16)
        for k in range(1, NY):
            send(u0, uy.at[k - 1], u_send.at[k - 1], u_recv.at[k - 1], y_peer[k])

    def up_y():
        for k in range(NY - 1):
            wait_for(uy.at[k], u_recv.at[k], u_send.at[0])
        u1[...] = add([u0[...], *(uy[k] for k in range(NY - 1))]).astype(bf16)
        for j in range(1, NX):
            send(u1, ux.at[j - 1], u_send.at[2 + j], u_recv.at[2 + j], x_peer[j])

    def up_x():
        for j in range(NX - 1):
            wait_for(ux.at[j], u_recv.at[3 + j], u_send.at[0])
        u2[...] = add([u1[...], *(ux[j] for j in range(NX - 1))]).astype(bf16)
        send(u2, us, u_send.at[6], u_recv.at[6], sib)

    def down_terms():
        wait_for(us, u_recv.at[6], u_send.at[0])
        sums = add([u2[...], us[...]])
        v = jnp.concatenate([sums[:docs], sums[docs:, : units - wide_half]], axis=1)
        critic_hidden = v / (1.0 + jnp.exp(-v))
        doc = lax.broadcasted_iota(jnp.int32, critic_hidden.shape, 0)
        rule = jnp.zeros(critic_hidden.shape, jnp.int32)
        for d in range(docs):
            rule = jnp.where(doc == d, rules[d], rule)
        down_copy.wait()
        total = None
        for r in range(down.shape[0]):
            mine = jnp.where(rule == r, critic_hidden, 0.0).astype(bf16)
            term = jnp.dot(mine, down[r], preferred_element_type=f32)
            total = term if total is None else total + term
        d0[...] = total
        send(d0, dh, d_send.at[0], d_recv.at[n_z], h_peer)

    def down_h():
        wait_for(dh, d_recv.at[n_z], d_send.at[0])
        both = d0[...] + dh[...]
        both = jnp.concatenate([both[:, :128], both[:, 128:]], axis=0).astype(bf16)
        d1[...] = both
        dz[z] = both
        for j in range(1, n_z):
            send(d1, dz.at[z], d_send.at[j], d_recv.at[z], z_peer[j])

    def down_z():
        for j in range(1, n_z):
            there = (z + j) % n_z
            wait_for(dz.at[there], d_recv.at[there], d_send.at[0])
        total = add([dz[a] for a in range(n_z)])
        critic_values[...] = jnp.concatenate([total[:docs], total[docs:]], axis=1).astype(bf16)

    kind = z % 2

    def product(a, weights):
        return jnp.dot(both[a].reshape(NC * tokens, depth), weights[a], preferred_element_type=f32)

    def use_w(a):
        acc_kv[...] += product(a, wkv).reshape(acc_kv.shape)

    def use_q(a):
        acc_q[...] += product(a, wq).reshape(acc_q.shape)

    def kv_part():
        send(acc_kv.at[1 - c], part_kv, swap.at[2], swap.at[3], sib)

    def kv_own_kind():
        wait_for(part_kv, swap.at[3], swap.at[2])
        kv[kind, s] = (acc_kv[c] + part_kv[...]).astype(bf16)
        send(kv.at[kind, s], kv.at[kind, s], kvz.at[0], kvz.at[1], z_mate)

    def other_kind():
        wait_for(kv.at[1 - kind, s], kvz.at[1], kvz.at[0])

    def q_part():
        send(acc_q.at[1 - c], part_q, swap.at[4], swap.at[5], sib)

    def q_sum():
        wait_for(part_q, swap.at[5], swap.at[4])

    groups = tuple(
        tuple(i for i, event in enumerate(RING_EVENTS) if event[1] == dy) for dy in (0, -1, 1, 2)
    )
    rows = QH_DEV * tokens
    chunk = KEY_CHUNK * tokens
    inverse_root = 1.0 / math.sqrt(128)

    def attend(g):
        for i in groups[g]:
            k_other(i)
            v_other(i)
        if g == 0:
            queries = (acc_q[c] + part_q[...]).astype(bf16)
            stacked[:tokens] = queries[:, :128]
            stacked[tokens:] = queries[:, 128:]
            maxima[...] = jnp.full_like(maxima, -1e30)
            totals[...] = jnp.zeros_like(totals)
            mixed[...] = jnp.zeros_like(mixed)
        dy = (0, -1, 1, 2)[g]
        chip_row = (y + dy + NY) % NY

        def step(i, carry):
            at = chip_row * (NX * NC) + i * KEY_CHUNK
            keys = kv[0, pl.ds(at, KEY_CHUNK)].reshape(chunk, 128)
            values = kv[1, pl.ds(at, KEY_CHUNK)].reshape(chunk, 128)
            position = lax.broadcasted_iota(jnp.int32, (rows, 1), 0) % tokens + first
            start = jnp.zeros((rows, 1), jnp.int32)
            for d in range(docs):
                start = jnp.maximum(start, jnp.where(ends[d] < position, ends[d] + 1, 0))
            found = lax.dot_general(
                stacked[...], keys, (((1,), (1,)), ((), ())), preferred_element_type=f32
            )
            there = lax.broadcasted_iota(jnp.int32, (rows, chunk), 1) + at * tokens
            allowed = (there >= start) & (there <= position)
            found = jnp.where(allowed, found * inverse_root, -1e30)
            old = maxima[...]
            new = jnp.maximum(old, jnp.max(found, axis=1, keepdims=True))
            weights = jnp.where(allowed, jnp.exp(found - new[:, :1]), 0.0)
            keep = jnp.exp(old - new)
            maxima[...] = new
            totals[...] = totals[...] * keep + jnp.sum(weights, axis=1, keepdims=True)
            mixed[...] = mixed[...] * keep + jnp.dot(
                weights.astype(bf16), values, preferred_element_type=f32
            )
            return carry

        steps = NX * NC // KEY_CHUNK
        if g == 0:
            lax.fori_loop(0, x * NC // KEY_CHUNK + 1, step, 0)
        else:

            @pl.when(chip_row < y)
            def _():
                lax.fori_loop(0, steps, step, 0)

    value_copy.wait()
    wq_copy.wait()
    waiting, ready = [], [False]

    def use(what, a):
        if ready[0]:
            what(a)
        else:
            waiting.append((what, a))

    stages = {
        "ends": end_rows, "norm": norm, "ey": end_rows_y, "ex": end_rows_x, "up": up_terms, "uy": up_y,
        "ux": up_x, "down": down_terms, "dh": down_h, "late": late, "both": other_rows, "kpart": kv_part,
        "kown": kv_own_kind, "z": other_kind, "qpart": q_part, "qown": q_sum,
        **{f"a{g}": functools.partial(attend, g) for g in range(4)}, "dz": down_z,
    }
    for step in SCHEDULE:
        if step in stages:
            stages[step]()
            if step == "both":
                ready[0] = True
                for what, a in waiting:
                    what(a)
            continue
        i = int(step[1:])
        if step[0] == "w":
            use(use_w, w_own(i))
        if step[0] == "q":
            use(use_q, q_own(i))
        if step[0] == "k":
            k_own(i)
        if step[0] == "v":
            v_own(i)
    out = (mixed[...] / totals[...]).astype(bf16)
    attention[:, :128] = out[:tokens]
    attention[:, 128:] = out[tokens:]
    for copy, when in sends:
        if when is None:
            copy.wait_send()
        else:
            pl.when(when)(copy.wait_send)


def hand_over(attention, critic_values, attention_out, critic_values_out):
    attention_out[...] = attention[...]
    critic_values_out[...] = critic_values[...]


def shards(
    hidden, norm_gain, w_query, w_key, w_value, doc_lengths, critic_up, critic_down, rule_ids
):
    tokens, width = hidden.shape
    depth, q_columns = w_query.shape
    rules, hidden_units, out_columns = critic_down.shape
    docs = doc_lengths.shape[0]
    n_seq = NY * NX * NC
    n_z = lax.axis_size("tp") // NH
    folded = (2 * docs, (hidden_units // 2 + 127) // 128 * 128)
    bf16, f32 = jnp.bfloat16, jnp.float32
    vmem, dma = pltpu.VMEM, pltpu.SemaphoreType.DMA
    anywhere = pl.BlockSpec(memory_space=pl.ANY)
    made = pl.pallas_call(
        kernel,
        out_shape=(
            jax.ShapeDtypeStruct((tokens, q_columns), bf16),
            jax.ShapeDtypeStruct((docs, out_columns), bf16),
        ),
        in_specs=[
            pl.BlockSpec(memory_space=pltpu.SMEM),
            pl.BlockSpec(memory_space=pltpu.SMEM),
            pl.BlockSpec(memory_space=pltpu.VMEM),
            *[anywhere] * 6,
        ],
        out_specs=(pl.BlockSpec(memory_space=pltpu.VMEM), pl.BlockSpec(memory_space=pltpu.VMEM)),
        scratch_shapes=[
            vmem((tokens, width), bf16),
            vmem((n_seq // NC, NC, tokens, depth), bf16),
            vmem((n_seq // NC, tokens, depth), bf16),
            vmem((n_seq // NC, depth, 128), bf16),
            vmem((n_seq // NC, depth, q_columns), bf16),
            vmem(critic_up.shape, bf16),
            vmem(critic_down.shape, bf16),
            vmem((2, n_seq, tokens, 128), bf16),
            vmem((NC, tokens, 128), f32),
            vmem((tokens, 128), f32),
            vmem((NC, tokens, q_columns), f32),
            vmem((tokens, q_columns), f32),
            vmem((QH_DEV * tokens, 128), bf16),
            *[vmem((QH_DEV * tokens, 128), f32)] * 3,
            vmem((NY, NX, NC * docs, depth), bf16),
            vmem((NY - 1, NX, NC * docs, depth), bf16),
            vmem((NX, NC * docs, depth), bf16),
            vmem((NX - 1, NC * docs, depth), bf16),
            vmem((NC * docs, depth), bf16),
            vmem((NC * docs, depth), bf16),
            vmem((docs, width), f32),
            vmem(folded, bf16),
            vmem((NY - 1, *folded), bf16),
            vmem(folded, bf16),
            vmem((NX - 1, *folded), bf16),
            vmem(folded, bf16),
            vmem(folded, bf16),
            vmem((docs, out_columns), f32),
            vmem((docs, out_columns), f32),
            vmem((2 * docs, out_columns // 2), bf16),
            vmem((n_z, 2 * docs, out_columns // 2), bf16),
            dma((5,)),
            *[dma((N_SENDS,)), dma((n_seq,))] * 4,
            dma((2,)),
            dma((6,)),
            dma((7,)),
            dma((7,)),
            dma((7,)),
            dma((7,)),
            dma((n_z,)),
            dma((n_z + 1,)),
        ],
        compiler_params=pltpu.CompilerParams(
            collective_id=0, has_side_effects=True, vmem_limit_bytes=60 * 1024 * 1024
        ),
        cost_estimate=pl.CostEstimate(
            flops=2 * 10**9, bytes_accessed=8 * 2**20, transcendentals=2**20
        ),
    )(
        doc_lengths, rule_ids, norm_gain, hidden, w_query, w_key, w_value,
        critic_up, critic_down,
    )
    inside = pl.BlockSpec(memory_space=pltpu.VMEM)
    return pl.pallas_call(
        hand_over,
        out_shape=tuple(jax.ShapeDtypeStruct(part.shape, part.dtype) for part in made),
        in_specs=[inside, inside],
        out_specs=(inside, inside),
    )(*made)


def solution(mesh):
    return jax.shard_map(
        shards,
        mesh=mesh,
        in_specs=(
            P("seq", None),
            P(),
            P("seq", "tp"),
            P("seq", None),
            P("seq", None),
            P(),
            P("seq", "tp"),
            P(None, "tp", "seq"),
            P(),
        ),
        out_specs=(P("seq", "tp"), P(None, "seq")),
        check_vma=False,
    )
```

time: 93 us -> 67.3 us (0.72)
  the two profiles are of different devices: /device:TPU:63 before, /device:TPU:56 now
where the time goes in v2:
time: 67.3 us; the launch traced here: 67.1 us
  Pallas kernels  66.4 us (99%)
    pallas_call x1, Pallas kernels, shards(): pl.pallas_call(kernel, out_shape=(jax.ShapeDtypeStruct((tokens, q_columns...  65 us
    pallas_call x1, Pallas kernels, shards(): pl.pallas_call(hand_over, out_shape=tuple((jax.ShapeDtypeStruct(part.shap...  1.48 us

profile of v2, /device:TPU:56, one launch (start us, length us, event | category | flops | bytes accessed | tf_op | source)
XLA Modules:
  0.0 67.1 jit_solution(10855960627705982167)
XLA Ops:
  0.6 65.0 %shard_map.104 = (bf16[128,256]{1,0:T(8,128)(2,1)}, bf16[8,256]{1,0:T(8,128)(2,1)}) custom-call(s32[8]{0:T(128)} %lens.1, s32[8]{0:T(128)} %rules.1, bf16[8192]{0:T(1024)(128)(2,1)} %gain.1, bf16[128,8192]{1,0:T(8,128)(2,1)} %hidden.1, bf16[256,256]{1,0:T(8,128)(2,1)} %w_query.1, bf16[256,768]{1,0:T(8,128)(2,1)} %w_key.1, bf16[256,768]{1,0:T(8,128)(2,1)} %w_value.1, ...), custom_call_target="tpu_custom_call" | custom-call | flops 2000000000 | bytes 8388608 | tf_op jit(solution)/shard_map/pallas_call | solution.py:497
  65.6 1.5 %shard_map.105 = (bf16[128,256]{1,0:T(8,128)(2,1)}, bf16[8,256]{1,0:T(8,128)(2,1)}) custom-call(bf16[128,256]{1,0:T(8,128)(2,1)} %get-tuple-element.4.attention, bf16[8,256]{1,0:T(8,128)(2,1)} %get-tuple-element.5.critic_values), custom_call_target="tpu_custom_call" | custom-call | tf_op jit(solution)/shard_map/pallas_call | solution.py:564

commit v3 on v2

--- a/solution.py
+++ b/solution.py
@@ -12,7 +12,6 @@
 GROUP = 8
 NY, NX, NC = 4, 4, 2
 NH = 2
-KEY_CHUNK = 4
 MESH = pl.DeviceIdType.MESH
 
 LINE_EVENTS = (
@@ -23,11 +22,13 @@
     (0, 0), (-1, 0), (1, 0), (0, -1), (0, 1), (2, 0), (-1, -1), (-1, 1),
     (1, -1), (1, 1), (2, -1), (2, 1), (0, 2), (1, 2), (-1, 2), (2, 2),
 )
+FAR = (0, -1, 1, 2)
+LAST_OF = tuple(max(i for i, event in enumerate(RING_EVENTS) if event[1] == b) for b in FAR)
 N_SENDS = 32
 SCHEDULE = (
     "w0", "q0", "ends", "w1", "w2", "w3", "late", "norm", "ey", "w4", "w5", "q1", "w6", "q2", "w7", "w8", "q3", "w9",
-    "q4", "ex", "up", "w10", "w11", "q5", "w12", "both", "w13", "w14", "w15", "kpart", "uy", "q6", "q7", "kown", "ux",
-    "z", "k0", "v0", "q8", "q9", "down", "k1", "k2", "q10", "v1", "v2", "q11", "v3", "q12", "q13", "k3", "k4", "k5",
+    "q4", "ex", "up", "w10", "w11", "q5", "w12", "both", "w13", "w14", "w15", "kpart", "uy", "q6", "q7", "kown", "k0",
+    "ux", "z", "v0", "q8", "q9", "down", "k1", "k2", "q10", "v1", "v2", "q11", "v3", "q12", "q13", "k3", "k4", "k5",
     "v4", "k6", "q14", "v5", "k7", "v6", "dh", "q15", "qpart", "k8", "v7", "k9", "v8", "k10", "k11", "v9", "k12",
     "v10", "v11", "v12", "qown", "a0", "k13", "v13", "v14", "k14", "a1", "k15", "v15", "a2", "a3", "dz",
 )
@@ -38,7 +39,7 @@
     attention, critic_values,
     hid, both, outbox, wkv, wq, up, down, kv, acc_kv, part_kv, acc_q, part_q, stacked, maxima, totals, mixed,
     e0, ey, e1, ex, e2, es, picked, u0, uy, u1, ux, u2, us, d0, dh, d1, dz,
-    local, w_send, w_recv, q_send, q_recv, k_send, k_recv, v_send, v_recv, kvz, swap,
+    local, w_send, w_recv, q_send, q_recv, k_send, k_recv, v_send, v_recv, k_swap, v_swap, kvz, swap,
     e_send, e_recv, u_send, u_recv, d_send, d_recv,
 ):
     f32, bf16 = jnp.float32, jnp.bfloat16
@@ -166,15 +167,18 @@
 
         return own
 
-    def ring_gather(buf, send_sems, recv_sems, x_first, cores):
+    def ring_gather(buf, send_sems, recv_sems, x_first, swap_sems=None):
         go, got = mover(buf, send_sems, recv_sems)
         near, far = ((x_next, x_back), (y_next, y_back)) if x_first else ((y_next, y_back), (x_next, x_back))
         half = buf.shape[1] // 2
 
         def place(a, b, core):
             dx, dy = (a, b) if x_first else (b, a)
-            at = (y + dy + NY) % NY * NX + column(dx)
-            return at * NC + core if cores else at
+            ay, ax = (y + dy + NY) % NY, column(dx)
+            return ay * NX + ax if swap_sems is None else (ay * NC + core) * NX + ax
+
+        def line_of(b, core):
+            return buf.at[pl.ds(((y + b + NY) % NY * NC + core) * NX, NX)]
 
         def own(i):
             a, b = RING_EVENTS[i]
@@ -193,21 +197,22 @@
                 go(shard, far[0])
             if b == 0 or (b == 1 and a in (-1, 2)):
                 go(shard, far[1])
-            if cores:
-                go(shard, sib)
+            if swap_sems is not None and i in LAST_OF:
+                g = LAST_OF.index(i)
+                line = line_of(FAR[g], c)
+                send(line, line, swap_sems.at[g], swap_sems.at[len(FAR) + g], sib)
             return shard
 
-        def other(i):
-            shard = place(*RING_EVENTS[i], 1 - c)
-            got(shard)
-            return shard
+        def other(g):
+            wait_for(line_of(FAR[g], 1 - c), swap_sems.at[len(FAR) + g], swap_sems.at[g])
 
         return own, other
 
-    w_own, _ = ring_gather(wkv, w_send, w_recv, False, False)
+    kind = z % 2
+    w_own, _ = ring_gather(wkv, w_send, w_recv, False)
     q_own = line_gather(wq, q_send, q_recv)
-    k_own, k_other = ring_gather(kv.at[0], k_send, k_recv, True, True)
-    v_own, v_other = ring_gather(kv.at[1], v_send, v_recv, True, True)
+    k_own, k_other = ring_gather(kv.at[kind], k_send, k_recv, True, k_swap)
+    v_own, v_other = ring_gather(kv.at[1 - kind], v_send, v_recv, True, v_swap)
     n_events = len(RING_EVENTS)
 
     acc_kv[...] = jnp.zeros_like(acc_kv)
@@ -350,7 +355,7 @@
         total = add([dz[a] for a in range(n_z)])
         critic_values[...] = jnp.concatenate([total[:docs], total[docs:]], axis=1).astype(bf16)
 
-    kind = z % 2
+    mine = (y * NC + c) * NX + x
 
     def product(a, weights):
         return jnp.dot(both[a].reshape(NC * tokens, depth), weights[a], preferred_element_type=f32)
@@ -366,11 +371,11 @@
 
     def kv_own_kind():
         wait_for(part_kv, swap.at[3], swap.at[2])
-        kv[kind, s] = (acc_kv[c] + part_kv[...]).astype(bf16)
-        send(kv.at[kind, s], kv.at[kind, s], kvz.at[0], kvz.at[1], z_mate)
+        kv[kind, mine] = (acc_kv[c] + part_kv[...]).astype(bf16)
+        send(kv.at[kind, mine], kv.at[kind, mine], kvz.at[0], kvz.at[1], z_mate)
 
     def other_kind():
-        wait_for(kv.at[1 - kind, s], kvz.at[1], kvz.at[0])
+        wait_for(kv.at[1 - kind, mine], kvz.at[1], kvz.at[0])
 
     def q_part():
         send(acc_q.at[1 - c], part_q, swap.at[4], swap.at[5], sib)
@@ -378,17 +383,13 @@
     def q_sum():
         wait_for(part_q, swap.at[5], swap.at[4])
 
-    groups = tuple(
-        tuple(i for i, event in enumerate(RING_EVENTS) if event[1] == dy) for dy in (0, -1, 1, 2)
-    )
     rows = QH_DEV * tokens
-    chunk = KEY_CHUNK * tokens
+    chunk = NX * tokens
     inverse_root = 1.0 / math.sqrt(128)
 
     def attend(g):
-        for i in groups[g]:
-            k_other(i)
-            v_other(i)
+        k_other(g)
+        v_other(g)
         if g == 0:
             queries = (acc_q[c] + part_q[...]).astype(bf16)
             stacked[:tokens] = queries[:, :128]
@@ -396,13 +397,12 @@
             maxima[...] = jnp.full_like(maxima, -1e30)
             totals[...] = jnp.zeros_like(totals)
             mixed[...] = jnp.zeros_like(mixed)
-        dy = (0, -1, 1, 2)[g]
-        chip_row = (y + dy + NY) % NY
+        chip_row = (y + FAR[g] + NY) % NY
 
         def step(i, carry):
-            at = chip_row * (NX * NC) + i * KEY_CHUNK
-            keys = kv[0, pl.ds(at, KEY_CHUNK)].reshape(chunk, 128)
-            values = kv[1, pl.ds(at, KEY_CHUNK)].reshape(chunk, 128)
+            at = (chip_row * NC + i) * NX
+            keys = kv[0, pl.ds(at, NX)].reshape(chunk, 128)
+            values = kv[1, pl.ds(at, NX)].reshape(chunk, 128)
             position = lax.broadcasted_iota(jnp.int32, (rows, 1), 0) % tokens + first
             start = jnp.zeros((rows, 1), jnp.int32)
             for d in range(docs):
@@ -410,7 +410,9 @@
             found = lax.dot_general(
                 stacked[...], keys, (((1,), (1,)), ((), ())), preferred_element_type=f32
             )
-            there = lax.broadcasted_iota(jnp.int32, (rows, chunk), 1) + at * tokens
+            there = lax.broadcasted_iota(jnp.int32, (1, chunk), 1)
+            chip = chip_row * NX + lax.div(there, tokens)
+            there = (chip * NC + i) * tokens + lax.rem(there, tokens)
             allowed = (there >= start) & (there <= position)
             found = jnp.where(allowed, found * inverse_root, -1e30)
             old = maxima[...]
@@ -424,14 +426,13 @@
             )
             return carry
 
-        steps = NX * NC // KEY_CHUNK
         if g == 0:
-            lax.fori_loop(0, x * NC // KEY_CHUNK + 1, step, 0)
+            lax.fori_loop(0, NC, step, 0)
         else:
 
             @pl.when(chip_row < y)
             def _():
-                lax.fori_loop(0, steps, step, 0)
+                lax.fori_loop(0, NC, step, 0)
 
     value_copy.wait()
     wq_copy.wait()
@@ -541,6 +542,8 @@
             vmem((n_z, 2 * docs, out_columns // 2), bf16),
             dma((5,)),
             *[dma((N_SENDS,)), dma((n_seq,))] * 4,
+            dma((8,)),
+            dma((8,)),
             dma((2,)),
             dma((6,)),
             dma((7,)),

time: 67.3 us -> 66.6 us (0.990)
  Pallas kernels: 66.4 us -> 65.4 us
    pallas_call x1, Pallas kernels: 65 us -> 64 us  [shards(): pl.pallas_call(kernel, out_shape=(jax.ShapeDtypeStruct((tokens, q_columns...]
where the time goes in v3:
time: 66.6 us; the launch traced here: 66.1 us
  Pallas kernels  65.4 us (98%)
    pallas_call x1, Pallas kernels, shards(): pl.pallas_call(kernel, out_shape=(jax.ShapeDtypeStruct((tokens, q_columns...  64 us
    pallas_call x1, Pallas kernels, shards(): pl.pallas_call(hand_over, out_shape=tuple((jax.ShapeDtypeStruct(part.shap...  1.48 us

profile of v3, /device:TPU:56, one launch (start us, length us, event | category | flops | bytes accessed | tf_op | source)
XLA Modules:
  0.0 66.1 jit_solution(5894765543405114417)
XLA Ops:
  0.6 64.0 %shard_map.104 = (bf16[128,256]{1,0:T(8,128)(2,1)}, bf16[8,256]{1,0:T(8,128)(2,1)}) custom-call(s32[8]{0:T(128)} %lens.1, s32[8]{0:T(128)} %rules.1, bf16[8192]{0:T(1024)(128)(2,1)} %gain.1, bf16[128,8192]{1,0:T(8,128)(2,1)} %hidden.1, bf16[256,256]{1,0:T(8,128)(2,1)} %w_query.1, bf16[256,768]{1,0:T(8,128)(2,1)} %w_key.1, bf16[256,768]{1,0:T(8,128)(2,1)} %w_value.1, ...), custom_call_target="tpu_custom_call" | custom-call | flops 2000000000 | bytes 8388608 | tf_op jit(solution)/shard_map/pallas_call | solution.py:498
  64.6 1.5 %shard_map.105 = (bf16[128,256]{1,0:T(8,128)(2,1)}, bf16[8,256]{1,0:T(8,128)(2,1)}) custom-call(bf16[128,256]{1,0:T(8,128)(2,1)} %get-tuple-element.4.attention, bf16[8,256]{1,0:T(8,128)(2,1)} %get-tuple-element.5.critic_values), custom_call_target="tpu_custom_call" | custom-call | tf_op jit(solution)/shard_map/pallas_call | solution.py:567
